TPU v7x, 512 devices: a whole 4x4x16 slice. The times are simulated.
512 devices in a mesh: dp: 4 (over y_hi, core), expert: 32 (over y_lo, z), tensor: 4 (over x).
Axes of the slice: x: 4, y: 4 (y_hi: 2, y_lo: 2; y = y_hi * 2 + y_lo), z: 16, core: 2. Of those that a mesh axis runs over, the one named last changes fastest.
Arguments:
- grad_out: bfloat16 [16384, 7168], P(('dp', 'expert'), 'tensor'), may hold values from -2 to 2
- routes: int32 [16384, 2], P(('dp', 'expert')), may hold values from 0 to 31, all different within a row; in each aligned block of 128 rows (0 to 127, 128 to 255, ...) at most 12 rows name the same one
- probs: bfloat16 [16384, 2], P(('dp', 'expert')), may hold values from 0.099609375 to 1
- hidden: bfloat16 [32, 1536, 2432], P('expert', 'tensor', 'dp'), may hold values from -6 to 6
- weight: bfloat16 [32, 2432, 7168], P('expert', 'dp', 'tensor'), may hold values from -0.0625 to 0.0625
Outputs:
- grad_hidden: bfloat16 [32, 1536, 2432], P('expert', 'tensor', 'dp')
- grad_probs: float32 [16384, 2], P(('dp', 'expert'))
Inputs may be any that keep to these rules, and one draw needn't show every extreme that they name: `routes`: among the 128 rows of one device's tokens no expert is named more than 12 times; the two experts of a token differ.
All inputs are finite; a program needn't handle non-finite values.
Results may differ from a plain program's by a relative error of at most 0.001.
Values may be sent and summed in bfloat16 or wider, within the bound.
A program may use at most 64 MiB of HBM per device.

v0:
```python
import jax
import jax.numpy as jnp
from jax import lax
from jax.sharding import PartitionSpec as P


def shards(grad_out, routes, probs, hidden, weight):
    tok_rows = routes.shape[0]
    expert_count = lax.axis_size("expert")
    group_count = lax.axis_size("dp")
    capacity = min(tok_rows, 3 * tok_rows // expert_count)
    pair_count = 2 * tok_rows
    flat_expert = routes.reshape(-1)
    onehot = (flat_expert[:, None] == jnp.arange(expert_count, dtype=jnp.int32)[None, :]).astype(
        jnp.float32
    )
    lower_mask = (jnp.arange(pair_count)[:, None] > jnp.arange(pair_count)[None, :]).astype(
        jnp.float32
    )
    before = jnp.dot(lower_mask, onehot, precision=lax.Precision.HIGHEST)
    slot_index = jnp.sum(before * onehot, axis=1).astype(jnp.int32)
    slot_key = flat_expert * capacity + slot_index
    select = slot_key[None, :] == jnp.arange(expert_count * capacity, dtype=jnp.int32)[:, None]
    token_rows = jnp.repeat(grad_out, 2, axis=0)
    send_dout = jnp.dot(
        select.astype(jnp.bfloat16), token_rows, preferred_element_type=jnp.float32
    ).astype(jnp.bfloat16)
    send_dout = send_dout.reshape(expert_count, capacity, -1)
    send_prob = jnp.dot(
        select.astype(jnp.float32),
        probs.reshape(-1).astype(jnp.float32),
        precision=lax.Precision.HIGHEST,
    )
    send_prob = send_prob.astype(jnp.bfloat16).reshape(expert_count, capacity)
    width = send_dout.shape[2]
    copies_dout = jnp.broadcast_to(
        send_dout[None], (group_count, expert_count, capacity, width)
    ).reshape(group_count * expert_count, capacity, width)
    copies_prob = jnp.broadcast_to(send_prob[None], (group_count, expert_count, capacity)).reshape(
        group_count * expert_count, capacity
    )
    recv_dout, recv_prob = (
        lax.all_to_all(copies_dout, ("dp", "expert"), split_axis=0, concat_axis=0, tiled=True),
        lax.all_to_all(copies_prob, ("dp", "expert"), split_axis=0, concat_axis=0, tiled=True),
    )
    slots_all = recv_dout.shape[0] * capacity
    dout_rows = recv_dout.reshape(slots_all, -1)
    prob_rows = recv_prob.reshape(slots_all)
    local_weight = weight[0]
    local_hidden = hidden[0]
    own_rows = local_hidden.shape[0]
    back_sum = lax.psum_scatter(
        jnp.einsum("sd,fd->sf", dout_rows, local_weight, preferred_element_type=jnp.float32),
        "tensor",
        scatter_dimension=0,
        tiled=True,
    )
    own_prob = lax.dynamic_slice_in_dim(prob_rows, lax.axis_index("tensor") * own_rows, own_rows, 0)
    grad_hidden = (own_prob.astype(jnp.float32)[:, None] * back_sum).astype(jnp.bfloat16)[None]
    partial_score = jnp.sum(local_hidden.astype(jnp.float32) * back_sum, axis=1)
    block_size = expert_count * capacity
    summed = lax.psum(partial_score, "dp")
    spread = lax.all_gather(summed, "tensor", axis=0, tiled=True)
    own_scores = lax.dynamic_slice_in_dim(spread, lax.axis_index("dp") * block_size, block_size, 0)
    returned = lax.all_to_all(
        own_scores.reshape(expert_count, capacity),
        "expert",
        split_axis=0,
        concat_axis=0,
        tiled=True,
    )
    grad_flat = jnp.dot(
        returned.reshape(-1), select.astype(jnp.float32), precision=lax.Precision.HIGHEST
    )
    grad_probs = grad_flat.reshape(tok_rows, 2)
    return (grad_hidden, grad_probs)


def solution(mesh):
    return jax.shard_map(
        shards,
        mesh=mesh,
        in_specs=(
            P(("dp", "expert"), "tensor"),
            P(("dp", "expert"), None),
            P(("dp", "expert"), None),
            P("expert", "tensor", "dp"),
            P("expert", "dp", "tensor"),
        ),
        out_specs=(P("expert", "tensor", "dp"), P(("dp", "expert"), None)),
        check_vma=False,
    )
```

profile of v0, /device:TPU:25, one launch (start us, length us, event | category | flops | bytes accessed | tf_op | source)
XLA Modules:
  0.0 473.3 jit_solution(2310199974035532312)
XLA Ops:
  7.2 0.0 copy-start
  7.2 0.0 reduce-scatter.2.cloned.1.call-start
  7.2 1.6 broadcast_in_dim.28
  8.9 1.3 reshape.73
  10.1 0.8 copy.27
  10.9 0.1 reshape.70
  11.1 0.2 fusion.2
  11.3 0.0 copy-start.5
  11.3 0.6 copy-done.5
  11.9 0.6 copy-done.3
  12.4 1.7 convolution_convert_fusion
  14.2 1.4 broadcast_in_dim.29
  15.6 2.1 broadcast_in_dim.30
  17.6 339.1 %all_to_all.23 = bf16[128,12,1792]{2,1,0:T(8,128)(2,1)} all-to-all(bf16[128,12,1792]{2,1,0:T(8,128)(2,1)S(1)} %bitcast.22), channel_id=1, replica_groups=mesh['dp'=4,'expert'=32,'tensor'=4] {'dp','expert'}, dimensions={0} | all-to-all | bytes 11010048 | tf_op jit(solution)/shard_map/all_to_all | solution.py:43
  356.8 9.3 %reshape.75 = bf16[1536,1792]{1,0:T(8,128)(2,1)} reshape(bf16[128,12,1792]{2,1,0:T(8,128)(2,1)} %all_to_all.23) | data formatting | bytes 11010048 | tf_op jit(solution)/shard_map/reshape | solution.py:47
  366.1 0.0 copy-done
  366.1 7.9 %fusion = f32[1536,608]{0,1:T(8,128)} fusion(bf16[1536,1792]{1,0:T(8,128)(2,1)} %reshape.75, bf16[1,608,1792]{2,1,0:T(8,128)(2,1)S(1)} %copy-done), kind=kOutput, calls=%fused_computation.1 | convolution fusion | flops 3347054592 | bytes 11419648 | tf_op jit(solution)/shard_map/sd,fd->sf/dot_general | solution.py:53
  374.1 0.0 copy-start.2
  374.1 0.0 reduce-scatter.2.cloned.1.call-update
  374.1 0.6 copy-done.7
  374.7 0.1 copy.28
  374.9 0.1 reshape.80
  375.0 0.0 copy-done.4
  375.0 0.2 convolution_reduce_fusion
  375.2 0.1 broadcast_in_dim.12
  375.3 0.1 copy.29
  375.4 0.1 all_to_all.15
  375.5 0.8 copy.30
  376.3 12.8 %all-to-all-start = ((bf16[128,1,12]{2,1,0:T(2,128)(2,1)}), bf16[128,1,12]{2,1,0:T(2,128)(2,1)S(1)}, u32[]{:S(2)}, u32[]{:S(2)}) async-start(bf16[128,1,12]{2,1,0:T(2,128)(2,1)} %copy.30), calls=%async_computation | async-start | bytes 131072 | tf_op jit(solution)/shard_map/all_to_all | solution.py:44
  389.1 0.0 copy-done.6
  389.2 0.1 convert_element_type.42
  389.3 0.1 copy.32
  389.4 12.6 %all-to-all-done = bf16[128,1,12]{2,1,0:T(2,128)(2,1)S(1)} async-done(((bf16[128,1,12]{2,1,0:T(2,128)(2,1)}), bf16[128,1,12]{2,1,0:T(2,128)(2,1)S(1)}, u32[]{:S(2)}, u32[]{:S(2)}) %all-to-all-start) | async-done | bytes 3104 | tf_op jit(solution)/shard_map/all_to_all | solution.py:44
  401.9 0.2 reduce.1
  402.1 0.1 reshape.72
  402.3 0.1 dynamic-slice_convert_fusion
  402.3 19.5 %reduce-scatter.2.cloned.1.call-done = f32[384,608]{0,1:T(8,128)} async-done(((f32[1536,608]{0,1:T(8,128)}), f32[384,608]{0,1:T(8,128)}) %reduce-scatter.2.cloned.1.call-update) | async-done | bytes 933904 | tf_op jit(solution)/shard_map/reduce_scatter | solution.py:52
  421.9 2.1 fusion.3
  424.0 7.1 %psum.7 = f32[384]{0:T(512)S(1)} all-reduce(f32[384]{0:T(512)S(1)} %get-tuple-element.2), channel_id=1, replica_groups=mesh['dp'=4,'expert'=32,'tensor'=4] {'dp'}, use_global_device_ids=true, to_apply=%region_3.0 | all-reduce | flops 384 | bytes 3072 | tf_op jit(solution)/shard_map/psum | solution.py:62
  431.1 8.1 %all-gather = f32[4,1,384]{2,1,0:T(1,128)S(1)} all-gather(f32[1,1,384]{2,1,0:T(1,128)S(1)} %reshape.78), channel_id=1, replica_groups=mesh['dp'=4,'expert'=32,'tensor'=4] {'tensor'}, dimensions={0}, use_global_device_ids=true | all-gather | bytes 7680 | tf_op jit(solution)/shard_map/all_gather | solution.py:63
  439.2 0.1 dynamic_slice.7
  439.2 0.7 all_to_all.18
  439.9 13.3 %all-to-all-start.2 = ((f32[32,1,12]{2,1,0:T(1,128)}), f32[32,1,12]{2,1,0:T(1,128)S(1)}, u32[]{:S(2)}, u32[]{:S(2)}) async-start(f32[32,1,12]{2,1,0:T(1,128)} %bitcast.4), calls=%async_computation.3 | async-start | bytes 32768 | tf_op jit(solution)/shard_map/all_to_all | solution.py:65
  453.2 11.0 %all-to-all-done.2 = f32[32,1,12]{2,1,0:T(1,128)S(1)} async-done(((f32[32,1,12]{2,1,0:T(1,128)}), f32[32,1,12]{2,1,0:T(1,128)S(1)}, u32[]{:S(2)}, u32[]{:S(2)}) %all-to-all-start.2) | async-done | bytes 1568 | tf_op jit(solution)/shard_map/all_to_all | solution.py:65
  464.2 0.5 broadcast.29
  464.8 0.7 reduce.7
  465.5 0.1 reshape.82
  465.6 0.9 fusion.6
  (14 shorter events, 0.1 us)
Async XLA Ops:
  7.2 359.0 %copy-start = (bf16[1,608,1792]{2,1,0:T(8,128)(2,1)S(1)}, bf16[1,608,1792]{2,1,0:T(8,128)(2,1)}, u32[]{:S(2)}) copy-start(bf16[1,608,1792]{2,1,0:T(8,128)(2,1)} %param.9) | copy-start | bytes 6537220
  7.2 414.7 %reduce-scatter.2.cloned.1.call-start = ((), (), s32[]{:S(2)}) async-start(), calls=%async_computation.4 | async-start | bytes 4669440 | tf_op jit(solution)/shard_map/reduce_scatter | solution.py:52
  11.3 0.6 copy-start.5
  11.9 0.6 copy-start.3
  374.1 0.7 copy-start.7
  374.1 0.9 copy-start.4
  374.1 15.1 %copy-start.6 = (f32[256]{0:T(256)S(1)}, f32[256]{0:T(256)}, u32[]{:S(2)}) copy-start(f32[256]{0:T(256)} %copy-done.5) | copy-start | bytes 3076
  374.1 47.8 %copy-start.1 = (bf16[1,384,608]{1,2,0:T(8,128)(2,1)S(1)}, bf16[1,384,608]{1,2,0:T(8,128)(2,1)}, u32[]{:S(2)}) copy-start(bf16[1,384,608]{1,2,0:T(8,128)(2,1)} %param.8) | copy-start | bytes 1400836
  374.1 79.1 %copy-start.2 = (s32[128,2]{0,1:T(2,128)S(1)}, s32[128,2]{0,1:T(2,128)}, u32[]{:S(2)}) copy-start(s32[128,2]{0,1:T(2,128)} %param.6) | copy-start | bytes 3076
  376.3 25.6 %all-to-all-start = ((bf16[128,1,12]{2,1,0:T(2,128)(2,1)}), bf16[128,1,12]{2,1,0:T(2,128)(2,1)S(1)}, u32[]{:S(2)}, u32[]{:S(2)}) async-start(bf16[128,1,12]{2,1,0:T(2,128)(2,1)} %copy.30), calls=%async_computation | async-start | bytes 131072 | tf_op jit(solution)/shard_map/all_to_all | solution.py:44
  439.9 24.3 %all-to-all-start.2 = ((f32[32,1,12]{2,1,0:T(1,128)}), f32[32,1,12]{2,1,0:T(1,128)S(1)}, u32[]{:S(2)}, u32[]{:S(2)}) async-start(f32[32,1,12]{2,1,0:T(1,128)} %bitcast.4), calls=%async_computation.3 | async-start | bytes 32768 | tf_op jit(solution)/shard_map/all_to_all | solution.py:65
Sparse Core Ops, SparseCore 0:
  374.2 47.5 reduce-scatter.1
where the time goes:
time: 480 us; the launch traced here: 473 us
  blocking collectives  354 us (74%)
  waiting for transfers between devices  43.1 us (9%)
  starting transfers between devices  26.1 us (5%)
  local copies, waits for them, and re-layouts  21.5 us (4%)
  between operations  14.2 us (3%)
  matrix products  11 us (2%)
    all_to_all x1, blocking collectives, shards(): lax.all_to_all(copies_dout, ('dp', 'expert'), split_axis=0, concat_axis=0...  339 us
    reduce_scatter x1, waiting for transfers between devices, shards(): lax.psum_scatter(jnp.einsum('sd,fd->sf', dout_rows, local_weight, preferr...  19.5 us
    all_to_all x1, starting transfers between devices, shards(): lax.all_to_all(own_scores.reshape(expert_count, capacity), 'expert', spli...  13.3 us
    all_to_all x1, starting transfers between devices, shards(): lax.all_to_all(copies_prob, ('dp', 'expert'), split_axis=0, concat_axis=0...  12.8 us
    all_to_all x1, waiting for transfers between devices, shards(): lax.all_to_all(copies_prob, ('dp', 'expert'), split_axis=0, concat_axis=0...  12.6 us
    all_to_all x1, waiting for transfers between devices, shards(): lax.all_to_all(own_scores.reshape(expert_count, capacity), 'expert', spli...  11 us
  transfers between devices with their start and end apart: 3, of which 3 were waited for; matrix products, arithmetic and copies ran while one was open for 0% of the time, Pallas kernels for 0%

commit v1 on v0

v1 whole, which is shorter than its diff:
```python
import jax
import jax.numpy as jnp
from jax import lax
from jax.experimental import pallas as pl
from jax.experimental.pallas import tpu as pltpu
from jax.sharding import PartitionSpec as P

MESH = pl.DeviceIdType.MESH
F32 = jnp.float32
BF16 = jnp.bfloat16

TOK = 128
CAP = 12
Z = 16
PAIRS = Z // 2
EXP = 2 * Z
D = 1792
HALF = D // 2
MSG = D + HALF
FFX = 608
FP = 640
SLOTS = 384
UNITS = 2 * PAIRS


def iota(shape, dim):
    return lax.broadcasted_iota(jnp.int32, shape, dim)


def dot(a, b, **kw):
    return jnp.dot(a, b, preferred_element_type=F32, **kw)


def dot_t(a, b):
    return lax.dot_general(a, b, (((1,), (1,)), ((), ())), preferred_element_type=F32)


def offset(k):
    half = lax.shift_right_logical(k + 1, 1)
    return jnp.where(lax.rem(k, 2) == 1, half, -half)


def kernel(
    grad_hbm, routes_ref, probs_ref, hidden_hbm, weight_hbm,
    gh_hbm, gp_ref,
    tokens, sel, send, recv, w_buf, h_buf, part, relay, fin, out_buf,
    prob_out, prob_in, prob_col, score, score_sum, score_in, table, hot, pick,
    local_sem, ex_send, ex_recv, z_send, z_recv, y_send, sib_send, x_recv,
    p_send, p_recv, xs_send, relay_recv, fin_recv, dp_send, dp_recv, s_send, s_recv,
):
    dp = lax.axis_index("dp")
    ex = lax.axis_index("expert")
    x = lax.axis_index("tensor")
    h, c = lax.div(dp, 2), lax.rem(dp, 2)
    l, z = lax.div(ex, Z), lax.rem(ex, Z)
    y = 2 * h + l
    pair = lax.div(z, 2)
    direct = c == l
    zi = jnp.where(direct, y, 4)
    sibling = (2 * h + 1 - c, ex, x)

    load_grad = pltpu.make_async_copy(grad_hbm, tokens.at[0], local_sem.at[0])
    load_w = pltpu.make_async_copy(weight_hbm.at[0], w_buf.at[pl.ds(0, FFX)], local_sem.at[1])
    load_h = pltpu.make_async_copy(hidden_hbm.at[0], h_buf, local_sem.at[2])
    load_grad.start()
    load_w.start()
    load_h.start()

    barrier = pltpu.get_barrier_semaphore()

    def greet(device):
        pl.semaphore_signal(barrier, inc=1, device_id=device, device_id_type=MESH)

    def greet_z(i, carry):
        greet((dp, l * Z + lax.rem(z + i, Z), x))
        return carry

    lax.fori_loop(1, Z, greet_z, 0)
    greet(sibling)
    greet((2 * (1 - h) + c, ex, x))
    greet((2 * (1 - h) + 1 - c, ex, x))
    greet((c, (1 - l) * Z + z, x))
    greet((2 + c, (1 - l) * Z + z, x))
    for i in range(1, 4):
        greet((dp, ex, lax.rem(x + i, 4)))
    twin = x == dp

    def greet_t(i, carry):
        @pl.when(jnp.logical_or(jnp.logical_not(twin), i != ex))
        def _():
            greet((x, i, dp))

        return carry

    lax.fori_loop(0, EXP, greet_t, 0)

    lane, sub = iota((TOK, TOK), 1), iota((TOK, TOK), 0)
    hot0 = (routes_ref[:, 0:1] == lane).astype(F32)
    hot1 = (routes_ref[:, 1:2] == lane).astype(F32)
    both = hot0 + hot1
    earlier = dot((sub > lane).astype(BF16), both.astype(BF16))
    number = jnp.where(both > 0, earlier + 1.0, 0.0)
    number_t = jnp.transpose(number).astype(BF16)

    def selection(lam):
        row, col = iota((SLOTS, TOK), 0), iota((SLOTS, TOK), 1)
        first = row < 16 * Z
        rest = row - 16 * Z
        zz = jnp.where(first, row >> 4, rest >> 3)
        g = jnp.where(first, (row >> 3) & 1, (rest >> 2) & 1)
        s = jnp.where(first, row & 7, 8 + (rest & 3))
        expand = jnp.logical_and(col == lam * Z + zz, g == c).astype(BF16)
        return (dot(expand, number_t) == (s + 1).astype(F32)).astype(BF16)

    sel[2] = selection(1 - c)
    sel[0] = selection(c)
    probs = probs_ref[...].astype(F32)
    prob_table = jnp.zeros((TOK, TOK), F32)
    for k, hk in enumerate((hot0, hot1)):
        slot = jnp.sum(hk * earlier, axis=1, keepdims=True)
        prob_table += dot(
            jnp.transpose(hk * probs[:, k : k + 1]).astype(BF16),
            (slot == lane.astype(F32)).astype(BF16),
        )
        hot[k] = hk
        pick[k] = (slot.astype(jnp.int32) + lax.rem(z, 4) * CAP == lane).astype(F32)
    for e in range(EXP):
        prob_out[e] = prob_table[e : e + 1, :]

    load_grad.wait()
    pl.semaphore_wait(barrier, jnp.where(twin, 54, 55))

    send_sel = pltpu.make_async_remote_copy(
        sel.at[2], sel.at[1], ex_send.at[0], ex_recv.at[0], device_id=sibling, device_id_type=MESH
    )
    send_tokens = pltpu.make_async_remote_copy(
        tokens.at[0], tokens.at[1], ex_send.at[1], ex_recv.at[1], device_id=sibling, device_id_type=MESH
    )
    send_sel.start()
    send_tokens.start()

    def scatter(source, index, target, sent, got):
        def one(n, carry):
            own = jnp.logical_and(twin, n == ex)

            @pl.when(own)
            def _():
                pltpu.make_async_copy(source.at[index(n)], target.at[ex], got).start()

            @pl.when(jnp.logical_not(own))
            def _():
                pltpu.make_async_remote_copy(
                    source.at[index(n)], target.at[ex], sent, got, device_id=(x, n, dp), device_id_type=MESH
                ).start()

            return carry

        lax.fori_loop(0, EXP, one, 0)

    def scatter_sent(target, sent):
        @pl.when(twin)
        def _():
            ref = target.at[pl.ds(0, EXP - 1)]
            pltpu.make_async_copy(ref, ref, sent).wait()

        @pl.when(jnp.logical_not(twin))
        def _():
            pltpu.make_async_copy(target, target, sent).wait()

    scatter(prob_out, lambda n: n, prob_in, p_send, p_recv)

    send_sel.wait_recv()
    send_tokens.wait_recv()
    for n in range(0, D, 256):
        block = dot(sel[0, 0 : 16 * Z], tokens[0, :, n : n + 256])
        block += dot(sel[1, 0 : 16 * Z], tokens[1, :, n : n + 256])
        send[:, :, n : n + 256] = block.reshape(Z, 16, 256).astype(BF16)
    for n in range(0, HALF, 128):
        halves = []
        for at in (n, HALF + n):
            block = dot(sel[0, 16 * Z :], tokens[0, :, at : at + 128])
            block += dot(sel[1, 16 * Z :], tokens[1, :, at : at + 128])
            halves.append(block.reshape(Z, 8, 128))
        send[:, :, D + n : D + n + 128] = jnp.concatenate(halves, axis=1).astype(BF16)

    def send_z(i, carry):
        to = 2 * lax.rem(pair + offset(lax.div(i, 2)) + PAIRS, PAIRS) + lax.rem(i, 2)

        @pl.when(to == z)
        def _():
            pltpu.make_async_copy(send.at[to], recv.at[zi, z], z_recv.at[z]).start()

        @pl.when(to != z)
        def _():
            pltpu.make_async_remote_copy(
                send.at[to], recv.at[zi, z], z_send, z_recv.at[z],
                device_id=(dp, l * Z + to, x), device_id_type=MESH,
            ).start()

        return carry

    lax.fori_loop(0, Z, send_z, 0)

    pltpu.make_async_copy(prob_in, prob_in, p_recv).wait()
    for e in range(EXP):
        table[e : e + 1, :] = prob_in[e]
    row, col = iota((SLOTS, EXP), 0), iota((SLOTS, EXP), 1)
    spread = dot(((row * 5462) >> 16 == col).astype(BF16), table[...].astype(BF16))
    row, col = iota((SLOTS, TOK), 0), iota((SLOTS, TOK), 1)
    mine = row - CAP * ((row * 5462) >> 16) == col
    prob_col[...] = jnp.broadcast_to(jnp.sum(jnp.where(mine, spread, 0.0), axis=1, keepdims=True), (SLOTS, TOK))
    w_buf[FFX:FP, :] = jnp.zeros((FP - FFX, D), BF16)
    load_w.wait()
    load_h.wait()

    def place(ys, rp):
        return recv.at[ys, pl.ds(2 * rp, 2)]

    def arrived(ys, rp):
        pltpu.make_async_copy(place(ys, rp), place(ys, rp), x_recv.at[ys, rp]).wait()

    def to_sibling(ys, rp):
        pltpu.make_async_remote_copy(
            place(ys, rp), place(ys, rp), sib_send.at[ys], x_recv.at[ys, rp],
            device_id=sibling, device_id_type=MESH,
        ).start()

    def along_y(i, rp, device):
        pltpu.make_async_remote_copy(
            place(zi, rp), place(y, rp), y_send.at[i], x_recv.at[y, rp], device_id=device, device_id_type=MESH
        ).start()

    def origin(k):
        return lax.rem(pair - offset(k) + PAIRS, PAIRS)

    def stage_z(k):
        rp = origin(k)
        for i in range(2):
            ref = recv.at[zi, 2 * rp + i]
            pltpu.make_async_copy(ref, ref, z_recv.at[2 * rp + i]).wait()

        @pl.when(direct)
        def _():
            along_y(0, rp, (2 * (1 - h) + c, ex, x))
            to_sibling(y, rp)

        @pl.when(jnp.logical_not(direct))
        def _():
            along_y(0, rp, (c, (1 - l) * Z + z, x))
            along_y(1, rp, (2 + c, (1 - l) * Z + z, x))

    def stage_y(k):
        rp = origin(k)

        @pl.when(direct)
        def _():
            for i in (1, 3, 2):
                ys = lax.rem(y + i, 4)
                arrived(ys, rp)
                to_sibling(ys, rp)

        @pl.when(jnp.logical_not(direct))
        def _():
            for ys in range(4):
                arrived(ys, rp)

    def along_x(i, source, target, got, device_x):
        pltpu.make_async_remote_copy(
            source, target, xs_send.at[i], got, device_id=(dp, ex, device_x), device_id_type=MESH
        ).start()

    def turn(lo):
        return 1 if lo == 0 else 3

    def compute(k):
        rp = origin(k)
        rows = [(lo, hi) for lo in range(2) for hi in range(2)]
        whole = [recv[2 * hi + lo, pl.ds(2 * rp, 2), :, 0:D].reshape(32, D) for lo, hi in rows]
        folded = [recv[2 * hi + lo, pl.ds(2 * rp, 2), :, D:MSG].reshape(32, HALF) for lo, hi in rows]
        first = jnp.concatenate([v[:, :HALF] for v in whole] + folded, axis=0)
        second = jnp.concatenate([v[:, HALF:] for v in whole] + folded, axis=0)
        for n0, n1 in ((0, 256), (256, 512), (512, 640)):
            left = dot_t(first, w_buf[n0:n1, :HALF])
            right = dot_t(second, w_buf[n0:n1, HALF:])
            low = iota((8, n1 - n0), 0) < 4
            for b, (lo, hi) in enumerate(rows):
                u = 2 * rp + lo
                ends = []
                for zz in range(2):
                    at = 32 * b + 16 * zz
                    for g in range(2):
                        v = left[at + 8 * g : at + 8 * g + 8] + right[at + 8 * g : at + 8 * g + 8]
                        part[u, 2 * hi + g, 8 * zz : 8 * zz + 8, n0:n1] = v
                    at += 128
                    ends.append(left[at : at + 8] + right[at + 8 : at + 16])
                part[u, 2 * hi, 16:24, n0:n1] = jnp.where(low, ends[0], pltpu.roll(ends[1], 4, 0))
                part[u, 2 * hi + 1, 16:24, n0:n1] = jnp.where(low, pltpu.roll(ends[0], 4, 0), ends[1])
        for lo in range(2):
            u, s = 2 * rp + lo, turn(lo)
            along_x(0, part.at[u, lax.rem(x + 2, 4)], relay.at[u], relay_recv.at[u], lax.rem(x + s, 4))
            back_x = lax.rem(x + 4 - s, 4)
            along_x(1, part.at[u, back_x], fin.at[1, u], fin_recv.at[1, u], back_x)

    def add_x(k):
        rp = origin(k)
        for lo in range(2):
            u = 2 * rp + lo
            to = lax.rem(x + turn(lo), 4)
            pltpu.make_async_copy(relay.at[u], relay.at[u], relay_recv.at[u]).wait()
            part[u, to] = part[u, to] + relay[u]
            along_x(2, part.at[u, to], fin.at[0, u], fin_recv.at[0, u], to)

    def step(k, carry):
        @pl.when(k < PAIRS)
        def _():
            stage_z(k)

        @pl.when(k >= 2)
        def _():
            add_x(k - 2)

        @pl.when(k >= 1)
        def _():
            stage_y(k - 1)
            compute(k - 1)

        return carry

    lax.fori_loop(0, PAIRS + 1, step, 0)
    add_x(PAIRS - 1)

    def wait_fin(u, carry):
        for i in range(2):
            pltpu.make_async_copy(fin.at[i, u], fin.at[i, u], fin_recv.at[i, u]).wait()
        return carry

    lax.fori_loop(0, UNITS, wait_fin, 0)

    def finish(q, carry):
        lo, j = lax.div(q, 4), lax.rem(q, 4)
        low = iota((8, FP), 0) < 4
        tiles = []
        for i in range(2):
            u = 2 * (2 * j + i) + lo
            total = part[u, x] + (fin[0, u] + fin[1, u])
            middle, end = pltpu.roll(total[8:16], 4, 0), total[16:24]
            tiles += [total[0:8], jnp.where(low, end, middle), jnp.where(low, middle, end)]
        back = jnp.concatenate(tiles, axis=0)[:, :FFX]
        rows = pl.ds(pl.multiple_of(48 * q, 16), 48)
        out_buf[rows, :] = (prob_col[rows, 0:1] * back).astype(BF16)
        col = jnp.sum(h_buf[rows, :].astype(F32) * back, axis=1, keepdims=True)
        score[dp, q] = jnp.sum(jnp.where(iota((48, TOK), 0) == iota((48, TOK), 1), col, 0.0), axis=0, keepdims=True)
        return carry

    lax.fori_loop(0, 8, finish, 0)
    store = pltpu.make_async_copy(out_buf, gh_hbm.at[0], local_sem.at[3])
    store.start()
    for i in range(1, 4):
        pltpu.make_async_remote_copy(
            score.at[dp], score.at[dp], dp_send, dp_recv,
            device_id=(lax.rem(dp + i, 4), ex, x), device_id_type=MESH,
        ).start()
    three = score.at[pl.ds(0, 3)]
    pltpu.make_async_copy(three, three, dp_recv).wait()
    score_sum[...] = (score[0] + score[1]) + (score[2] + score[3])
    scatter(score_sum, lambda n: lax.div(n, 4), score_in, s_send, s_recv)
    pltpu.make_async_copy(score_in, score_in, s_recv).wait()
    for e in range(EXP):
        table[e : e + 1, :] = score_in[e]
    for k in range(2):
        rows = dot(hot[k, :, 0:EXP], table[...], precision=lax.Precision.HIGHEST)
        gp_ref[:, k : k + 1] = jnp.sum(rows * pick[k], axis=1, keepdims=True)

    send_sel.wait_send()
    send_tokens.wait_send()
    scatter_sent(prob_in, p_send)
    scatter_sent(score_in, s_send)
    sent = send.at[pl.ds(0, Z - 1)]
    pltpu.make_async_copy(sent, sent, z_send).wait()
    pltpu.make_async_copy(send, send, y_send.at[0]).wait()

    @pl.when(direct)
    def _():
        for ys in range(4):
            pltpu.make_async_copy(send, send, sib_send.at[ys]).wait()

    @pl.when(jnp.logical_not(direct))
    def _():
        pltpu.make_async_copy(send, send, y_send.at[1]).wait()

    for i in range(3):
        pltpu.make_async_copy(relay, relay, xs_send.at[i]).wait()
    pltpu.make_async_copy(three, three, dp_send).wait()
    store.wait()


def shards(grad_out, routes, probs, hidden, weight):
    dma = pltpu.SemaphoreType.DMA
    vmem, hbm = pl.BlockSpec(memory_space=pltpu.VMEM), pl.BlockSpec(memory_space=pl.ANY)
    return pl.pallas_call(
        kernel,
        out_shape=(
            jax.ShapeDtypeStruct((1, SLOTS, FFX), BF16),
            jax.ShapeDtypeStruct((TOK, 2), F32),
        ),
        in_specs=[hbm, vmem, vmem, hbm, hbm],
        out_specs=(hbm, vmem),
        scratch_shapes=[
            pltpu.VMEM((2, TOK, D), BF16),
            pltpu.VMEM((3, SLOTS, TOK), BF16),
            pltpu.VMEM((Z, 16, MSG), BF16),
            pltpu.VMEM((5, Z, 16, MSG), BF16),
            pltpu.VMEM((FP, D), BF16),
            pltpu.VMEM((SLOTS, FFX), BF16),
            pltpu.VMEM((UNITS, 4, 24, FP), F32),
            pltpu.VMEM((UNITS, 24, FP), F32),
            pltpu.VMEM((2, UNITS, 24, FP), F32),
            pltpu.VMEM((SLOTS, FFX), BF16),
            pltpu.VMEM((EXP, 1, TOK), F32),
            pltpu.VMEM((EXP, 1, TOK), F32),
            pltpu.VMEM((SLOTS, TOK), F32),
            pltpu.VMEM((4, 8, 1, TOK), F32),
            pltpu.VMEM((8, 1, TOK), F32),
            pltpu.VMEM((EXP, 1, TOK), F32),
            pltpu.VMEM((EXP, TOK), F32),
            pltpu.VMEM((2, TOK, TOK), F32),
            pltpu.VMEM((2, TOK, TOK), F32),
            dma((4,)),
            dma((2,)),
            dma((2,)),
            dma,
            dma((Z,)),
            dma((2,)),
            dma((4,)),
            dma((4, PAIRS)),
            dma,
            dma,
            dma((3,)),
            dma((UNITS,)),
            dma((2, UNITS)),
            dma,
            dma,
            dma,
            dma,
        ],
        compiler_params=pltpu.CompilerParams(
            collective_id=0, has_side_effects=True, vmem_limit_bytes=48 * 1024 * 1024
        ),
        name="moe_down_backward",
    )(grad_out, routes, probs, hidden, weight)


def solution(mesh):
    return jax.shard_map(
        shards,
        mesh=mesh,
        in_specs=(
            P(("dp", "expert"), "tensor"),
            P(("dp", "expert"), None),
            P(("dp", "expert"), None),
            P("expert", "tensor", "dp"),
            P("expert", "dp", "tensor"),
        ),
        out_specs=(P("expert", "tensor", "dp"), P(("dp", "expert"), None)),
        check_vma=False,
    )
```

time: 480 us -> 134 us (0.28); the launches traced: 473 us -> 134 us
  blocking collectives: 354 us -> 0 us
  Pallas kernels: 0 us -> 126 us
  waiting for transfers between devices: 43.1 us -> 0 us
  starting transfers between devices: 26.1 us -> 0 us
  local copies, waits for them, and re-layouts: 21.5 us -> 7.08 us
  between operations: 14.2 us -> 0.65 us
  matrix products: 11 us -> 0 us
    all_to_all x1 -> x0, blocking collectives: 339 us -> none  [shards(): lax.all_to_all(copies_dout, ('dp', 'expert'), split_axis=0, concat_axis=0...]
    pallas_call x0 -> x1, Pallas kernels: none -> 126 us  [shards(): pl.pallas_call(kernel, out_shape=(jax.ShapeDtypeStruct((1, SLOTS, FFX), B...]
    all_to_all x2 -> x0, starting transfers between devices: 26.1 us -> none  [the longest x1 13.3 us: shards(): lax.all_to_all(own_scores.reshape(expert_count, capacity), 'expert', spli...]
    all_to_all x2 -> x0, waiting for transfers between devices: 23.6 us -> none  [the longest x1 12.6 us: shards(): lax.all_to_all(copies_prob, ('dp', 'expert'), split_axis=0, concat_axis=0...]
    reduce_scatter x1 -> x0, waiting for transfers between devices: 19.5 us -> none  [shards(): lax.psum_scatter(jnp.einsum('sd,fd->sf', dout_rows, local_weight, preferr...]
    reshape x6 -> x0, local copies, waits for them, and re-layouts: 11.1 us -> none  [the longest x1 9.34 us: shards(): dout_rows = recv_dout.reshape(slots_all, -1)]
    dot_general x5 -> x0, matrix products: 11 us -> none  [the longest x1 7.93 us: shards(): jnp.einsum('sd,fd->sf', dout_rows, local_weight, preferred_element_type=j...]
    all_gather x1 -> x0, blocking collectives: 8.06 us -> none  [shards(): spread = lax.all_gather(summed, 'tensor', axis=0, tiled=True)]
  transfers between devices with their start and end apart: 3 -> 0, of which waited for: 3 -> 0; matrix products, arithmetic and copies ran while one was open for 0% -> 0% of each run, Pallas kernels for 0% -> 0%
where the time goes in v1:
time: 134 us
  Pallas kernels  126 us (94%)
  local copies, waits for them, and re-layouts  7.08 us (5%)
    pallas_call x1, Pallas kernels, shards(): pl.pallas_call(kernel, out_shape=(jax.ShapeDtypeStruct((1, SLOTS, FFX), B...  126 us
    unnamed x7, local copies, waits for them, and re-layouts  5.46 us

profile of v1, /device:TPU:25, one launch (start us, length us, event | category | flops | bytes accessed | tf_op | source)
XLA Modules:
  0.0 133.8 jit_solution(10230705654700814083)
XLA Ops:
  0.6 0.8 copy.8.probs_ref
  1.4 0.8 copy.7.routes_ref
  2.2 1.3 copy.9.hidden_hbm
  3.5 0.0 copy-start
  3.5 1.6 %copy-done = bf16[1,608,1792]{2,1,0:T(8,128)(2,1)S(1)} copy-done((bf16[1,608,1792]{2,1,0:T(8,128)(2,1)S(1)}, bf16[1,608,1792]{2,1,0:T(8,128)(2,1)}, u32[]{:S(2)}) %copy-start) | copy-done | bytes 2179096
  5.1 0.0 copy-start.1
  5.1 1.0 copy-done.1
  6.1 126.1 %moe_down_backward.1 = (bf16[1,384,608]{2,1,0:T(8,128)(2,1)S(1)}, f32[128,2]{1,0:T(8,128)S(1)}) custom-call(bf16[128,1792]{1,0:T(8,128)(2,1)S(1)} %copy-done.1, s32[128,2]{1,0:T(8,128)S(1)} %copy.7.routes_ref, bf16[128,2]{1,0:T(8,128)(2,1)S(1)} %copy.8.probs_ref, bf16[1,384,608]{2,1,0:T(8,128)(2,1)S(1)} %copy.9.hidden_hbm, bf16[1,608,1792]{2,1,0:T(8,128)(2,1)S(1)} %copy-done), custom_call_target="tpu_custom_call" | custom-call | tf_op jit(solution)/shard_map/moe_down_backward/pallas_call | solution.py:400
  132.2 1.0 copy.10
  133.2 0.6 copy.11
Async XLA Ops:
  3.5 1.6 %copy-start = (bf16[1,608,1792]{2,1,0:T(8,128)(2,1)S(1)}, bf16[1,608,1792]{2,1,0:T(8,128)(2,1)}, u32[]{:S(2)}) copy-start(bf16[1,608,1792]{2,1,0:T(8,128)(2,1)} %weight_hbm.1) | copy-start | bytes 6537220
  5.1 1.0 copy-start.1

commit v2 on v0

v2 whole, which is shorter than its diff:
```python
import jax
import jax.numpy as jnp
from jax import lax
from jax.experimental import pallas as pl
from jax.experimental.pallas import tpu as pltpu
from jax.sharding import PartitionSpec as P

ORDER = (0, 1, -1, 2, -2, 3, -3, 4)
AHEAD = 3
SEQ = "ZYCAFG"
LAGS = dict(Z=0, Y=1, C=1, A=2, F=3, G=4)
MESH = pl.DeviceIdType.MESH
F32 = jnp.float32
BF16 = jnp.bfloat16

TOK = 128
CAP = 12
Z = 16
PAIRS = Z // 2
EXP = 2 * Z
D = 1792
HALF = D // 2
MSG = D + HALF
FFX = 608
FP = 640
SLOTS = 384
UNITS = 2 * PAIRS


def iota(shape, dim):
    return lax.broadcasted_iota(jnp.int32, shape, dim)


def dot(a, b, **kw):
    return jnp.dot(a, b, preferred_element_type=F32, **kw)


def dot_t(a, b):
    return lax.dot_general(a, b, (((1,), (1,)), ((), ())), preferred_element_type=F32)


def offset(k):
    at = ORDER[0]
    for i, o in enumerate(ORDER[1:], 1):
        at = jnp.where(k == i, o, at)
    return at


def turn(lo):
    return 1 if lo == 0 else 3


def kernel(
    grad_hbm, routes_ref, probs_ref, hidden_hbm, weight_hbm,
    gh_hbm, gp_ref,
    tokens, send, zbuf, other, recv, w_buf, h_buf, hidden, part, relay, fin, result, out_buf,
    prob_out, prob_in, prob_col, score, score_sum, score_in, table, hot, slots,
    local_sem, z_send, z_recv, y_send, sib_send, x_recv,
    p_send, p_recv, xs_send, relay_recv, fin_recv, dp_send, dp_recv, s_send, s_recv,
):
    dp = lax.axis_index("dp")
    ex = lax.axis_index("expert")
    x = lax.axis_index("tensor")
    h, c = lax.div(dp, 2), lax.rem(dp, 2)
    l, z = lax.div(ex, Z), lax.rem(ex, Z)
    y = 2 * h + l
    pair = lax.div(z, 2)
    sibling = (2 * h + 1 - c, ex, x)
    opposite = (2 * (1 - h) + c, ex, x)
    beside = ((c, (1 - l) * Z + z, x), (2 + c, (1 - l) * Z + z, x))

    load_grad = pltpu.make_async_copy(grad_hbm, tokens, local_sem.at[0])
    load_w = pltpu.make_async_copy(weight_hbm.at[0], w_buf.at[pl.ds(0, FFX)], local_sem.at[1])
    load_h = pltpu.make_async_copy(hidden_hbm.at[0], h_buf.at[pl.ds(0, FFX)], local_sem.at[2])
    load_grad.start()
    load_w.start()
    load_h.start()

    barrier = pltpu.get_barrier_semaphore()

    def greet(device):
        pl.semaphore_signal(barrier, inc=1, device_id=device, device_id_type=MESH)

    def greet_z(i, carry):
        greet((dp, l * Z + lax.rem(z + i, Z), x))
        return carry

    lax.fori_loop(1, Z, greet_z, 0)
    greet(sibling)
    greet(opposite)
    greet((2 * (1 - h) + 1 - c, ex, x))
    greet(beside[0])
    greet(beside[1])
    for i in range(1, 4):
        greet((dp, ex, lax.rem(x + i, 4)))
    twin = x == dp

    def greet_t(i, carry):
        @pl.when(jnp.logical_or(jnp.logical_not(twin), i != ex))
        def _():
            greet((x, i, dp))

        return carry

    lax.fori_loop(0, EXP, greet_t, 0)

    expert = iota((EXP, TOK), 0)
    hots = [(routes_ref[k : k + 1, :] == expert).astype(F32) for k in range(2)]
    both = hots[0] + hots[1]
    before = (iota((TOK, TOK), 0) < iota((TOK, TOK), 1)).astype(BF16)
    earlier = dot(both.astype(BF16), before)
    number = jnp.where(both > 0, earlier + 1.0, 0.0).astype(BF16)
    row, col = iota((SLOTS, EXP), 0), iota((SLOTS, EXP), 1)
    first, rest = row < 16 * Z, row - 16 * Z
    zz = jnp.where(first, row >> 4, rest >> 3)
    lam = jnp.where(first, (row >> 3) & 1, (rest >> 2) & 1)
    spread = dot((col == lam * Z + zz).astype(BF16), number)
    row = iota((SLOTS, TOK), 0)
    slot = jnp.where(row < 16 * Z, row & 7, 8 + (row & 3))
    select = (spread == (slot + 1).astype(F32)).astype(BF16)

    load_grad.wait()
    for n in range(0, D, 256):
        block = dot(select[0 : 16 * Z], tokens[:, n : n + 256])
        send[:, :, n : n + 256] = block.reshape(Z, 16, 256).astype(BF16)
    for n in range(0, HALF, 128):
        halves = []
        for at in (n, HALF + n):
            block = dot(select[16 * Z :], tokens[:, at : at + 128])
            halves.append(block.reshape(Z, 8, 128))
        send[:, :, D + n : D + n + 128] = jnp.concatenate(halves, axis=1).astype(BF16)

    pl.semaphore_wait(barrier, jnp.where(twin, 54, 55))

    def send_z(k):
        for i in range(2):
            to = 2 * lax.rem(pair + offset(k) + PAIRS, PAIRS) + i

            @pl.when(to == z)
            def _():
                pltpu.make_async_copy(send.at[to], zbuf.at[z], z_recv.at[z]).start()

            @pl.when(to != z)
            def _():
                pltpu.make_async_remote_copy(
                    send.at[to], zbuf.at[z], z_send, z_recv.at[z],
                    device_id=(dp, l * Z + to, x), device_id_type=MESH,
                ).start()

    def send_first(k, carry):
        send_z(k)
        return carry

    lax.fori_loop(0, AHEAD, send_first, 0)

    def small(source, target, n, sent, got):
        own = jnp.logical_and(twin, n == ex)

        @pl.when(own)
        def _():
            pltpu.make_async_copy(source, target, got).start()

        @pl.when(jnp.logical_not(own))
        def _():
            pltpu.make_async_remote_copy(
                source, target, sent, got, device_id=(x, n, dp), device_id_type=MESH
            ).start()

    def small_sent(target, sent):
        @pl.when(twin)
        def _():
            ref = target.at[pl.ds(0, EXP - 1)]
            pltpu.make_async_copy(ref, ref, sent).wait()

        @pl.when(jnp.logical_not(twin))
        def _():
            pltpu.make_async_copy(target, target, sent).wait()

    probs = probs_ref[...].astype(F32)
    weights = jnp.zeros((EXP, TOK), F32)
    for k in range(2):
        at = jnp.sum(hots[k] * earlier, axis=0, keepdims=True).astype(jnp.int32)
        weights += dot_t(
            (hots[k] * probs[k : k + 1, :]).astype(BF16), (iota((TOK, TOK), 0) == at).astype(BF16)
        )
        hot[k] = hots[k]
        slots[k] = jnp.broadcast_to(at + lax.rem(z, 2) * CAP, (8, TOK))
    for e in range(EXP):
        prob_out[e] = weights[e : e + 1, :]

    def send_prob(n, carry):
        small(prob_out.at[n], prob_in.at[ex], n, p_send, p_recv)
        return carry

    lax.fori_loop(0, EXP, send_prob, 0)

    h_buf[FFX:FP, :] = jnp.zeros((FP - FFX, SLOTS), BF16)
    w_buf[FFX:FP, :] = jnp.zeros((FP - FFX, D), BF16)
    table[...] = jnp.zeros((TOK, TOK), F32)
    load_h.wait()
    for i in range(0, SLOTS, 128):
        for j in range(0, FP, 128):
            hidden[i : i + 128, j : j + 128] = jnp.transpose(h_buf[j : j + 128, i : i + 128].astype(F32))
    load_w.wait()

    def take_prob():
        pltpu.make_async_copy(prob_in, prob_in, p_recv).wait()
        for e in range(EXP):
            table[e : e + 1, :] = prob_in[e]
        row, col = iota((SLOTS, EXP), 0), iota((SLOTS, EXP), 1)
        spread = dot(((row * 5462) >> 16 == col).astype(BF16), table[0:EXP].astype(BF16))
        row, col = iota((SLOTS, TOK), 0), iota((SLOTS, TOK), 1)
        mine = row - CAP * ((row * 5462) >> 16) == col
        prob_col[...] = jnp.broadcast_to(jnp.sum(jnp.where(mine, spread, 0.0), axis=1, keepdims=True), (SLOTS, TOK))

    def origin(k):
        return lax.rem(pair - offset(k) + PAIRS, PAIRS)

    def forward(source, core, ys, rp, sent, device):
        pltpu.make_async_remote_copy(
            source, recv.at[core, ys, rp], sent, x_recv.at[core, ys, rp], device_id=device, device_id_type=MESH
        ).start()

    def arrived(core, ys, rp):
        ref = recv.at[core, ys, rp]
        pltpu.make_async_copy(ref, ref, x_recv.at[core, ys, rp]).wait()

    def stage_z(k):
        rp = origin(k)
        for i in range(2):
            ref = zbuf.at[2 * rp + i]
            pltpu.make_async_copy(ref, ref, z_recv.at[2 * rp + i]).wait()
        both = zbuf[pl.ds(2 * rp, 2)].reshape(32, MSG)
        row, col = iota((32, 32), 0), iota((32, 32), 1)
        v = jnp.where(row < 16, l, 1 - l)
        eight, four = row & 7, row & 3
        whole = dot((col == 16 * ((row >> 3) & 1) + 8 * v + eight).astype(BF16), both[:, :D]).astype(BF16)
        at = 16 * ((eight >> 2) & 1) + 8 * ((row >> 3) & 1) + 4 * v + four
        folded = dot((col == at).astype(BF16), both[:, D:]).astype(BF16)
        recv[c, y, rp, :, 0:D] = whole[0:16]
        recv[c, y, rp, :, D:MSG] = folded[0:16]
        other[rp, :, 0:D] = whole[16:32]
        other[rp, :, D:MSG] = folded[16:32]
        forward(other.at[rp], c, y, rp, y_send.at[0], beside[0])
        forward(other.at[rp], c, y, rp, y_send.at[1], beside[1])
        forward(recv.at[c, y, rp], c, y, rp, y_send.at[2], opposite)
        forward(recv.at[c, y, rp], c, y, rp, sib_send.at[y], sibling)

    def stage_y(k):
        rp = origin(k)
        for i in (1, 3, 2):
            ys = lax.rem(y + i, 4)
            arrived(c, ys, rp)
            forward(recv.at[c, ys, rp], c, ys, rp, sib_send.at[ys], sibling)

    def along_x(i, source, target, got, device_x):
        pltpu.make_async_remote_copy(
            source, target, xs_send.at[i], got, device_id=(dp, ex, device_x), device_id_type=MESH
        ).start()

    def compute(k):
        rp = origin(k)
        for ys in range(4):
            arrived(1 - c, ys, rp)
        rows = [(lo, hi, core) for lo in range(2) for hi in range(2) for core in range(2)]
        whole = [recv[core, 2 * hi + lo, rp, :, 0:D] for lo, hi, core in rows]
        folded = [recv[core, 2 * hi + lo, rp, :, D:MSG] for lo, hi, core in rows]
        left_rows = jnp.concatenate([v[:, :HALF] for v in whole] + folded, axis=0)
        right_rows = jnp.concatenate([v[:, HALF:] for v in whole] + folded, axis=0)
        for n0, n1 in ((0, 256), (256, 512), (512, 640)):
            left = dot_t(left_rows, w_buf[n0:n1, :HALF])
            right = dot_t(right_rows, w_buf[n0:n1, HALF:])
            for i, (lo, hi, core) in enumerate(rows):
                at = 16 * i
                part[2 * rp + lo, 2 * hi + core, 0:16, n0:n1] = left[at : at + 16] + right[at : at + 16]
                at += 128
                part[2 * rp + lo, 2 * hi + core, 16:24, n0:n1] = left[at : at + 8] + right[at + 8 : at + 16]
        for lo in range(2):
            u, s = 2 * rp + lo, turn(lo)
            along_x(0, part.at[u, lax.rem(x + 2, 4)], relay.at[u], relay_recv.at[u], lax.rem(x + s, 4))
            back_x = lax.rem(x + 4 - s, 4)
            along_x(1, part.at[u, back_x], fin.at[1, u], fin_recv.at[1, u], back_x)

    def add_x(k):
        rp = origin(k)
        for lo in range(2):
            u = 2 * rp + lo
            to = lax.rem(x + turn(lo), 4)
            pltpu.make_async_copy(relay.at[u], relay.at[u], relay_recv.at[u]).wait()
            part[u, to] = part[u, to] + relay[u]
            along_x(2, part.at[u, to], fin.at[0, u], fin_recv.at[0, u], to)

    def finish(k):
        rp = origin(k)
        for lo in range(2):
            u = 2 * rp + lo
            for i in range(2):
                pltpu.make_async_copy(fin.at[i, u], fin.at[i, u], fin_recv.at[i, u]).wait()
            total = part[u, x] + (fin[0, u] + fin[1, u])
            low = iota((8, FP), 0) < 4
            middle, end = pltpu.roll(total[8:16], 4, 0), total[16:24]
            total = jnp.concatenate(
                [total[0:8], jnp.where(low, end, middle), jnp.where(low, middle, end)], axis=0
            )
            rows = pl.ds(pl.multiple_of(192 * lo + 24 * rp, 8), 24)
            result[rows, :] = prob_col[rows, 0:1] * total
            col = jnp.sum(hidden[rows, :] * total, axis=1, keepdims=True)
            score[dp, u] = jnp.sum(
                jnp.where(iota((24, TOK), 0) == iota((24, TOK), 1), col, 0.0), axis=0, keepdims=True
            )
        ref = score.at[dp, pl.ds(2 * rp, 2)]
        for i in range(1, 4):
            pltpu.make_async_remote_copy(
                ref, ref, dp_send, dp_recv.at[rp], device_id=(lax.rem(dp + i, 4), ex, x), device_id_type=MESH
            ).start()

    def give(k):
        rp = origin(k)
        three = score.at[0, pl.ds(0, 6)]
        pltpu.make_async_copy(three, three, dp_recv.at[rp]).wait()
        for lo in range(2):
            u = 2 * rp + lo
            score_sum[u] = (score[0, u] + score[1, u]) + (score[2, u] + score[3, u])
            for i in range(2):
                small(score_sum.at[u], score_in.at[ex], lo * Z + 2 * rp + i, s_send, s_recv)

    named = dict(Z=stage_z, Y=stage_y, C=compute, A=add_x, F=finish, G=give)
    stages = [(named[n], LAGS[n]) for n in SEQ]

    def step(k, carry):
        @pl.when(k < PAIRS - AHEAD)
        def _():
            send_z(k + AHEAD)

        @pl.when(k == LAGS["F"] - 1)
        def _():
            take_prob()

        for stage, lag in stages:

            @pl.when(jnp.logical_and(k >= lag, k < PAIRS + lag))
            def _(stage=stage, lag=lag):
                stage(k - lag)

        return carry

    lax.fori_loop(0, PAIRS + max(LAGS.values()), step, 0)

    for i in range(0, SLOTS, 128):
        for j in range(0, FP, 128):
            out_buf[j : j + 128, i : i + 128] = jnp.transpose(result[i : i + 128, j : j + 128]).astype(BF16)
    store = pltpu.make_async_copy(out_buf.at[pl.ds(0, FFX)], gh_hbm.at[0], local_sem.at[3])
    store.start()

    pltpu.make_async_copy(score_in, score_in, s_recv).wait()
    for e in range(EXP):
        table[e : e + 1, :] = score_in[e]
    by_lane = jnp.transpose(table[...])[:, 0:EXP]
    for k in range(2):
        spread = dot(by_lane, hot[k], precision=lax.Precision.HIGHEST)
        mine = iota((TOK, TOK), 0) == slots[k, 0:1, :]
        gp_ref[k : k + 1, :] = jnp.sum(jnp.where(mine, spread, 0.0), axis=0, keepdims=True)

    small_sent(prob_in, p_send)
    small_sent(score_in, s_send)
    sent = send.at[pl.ds(0, Z - 1)]
    pltpu.make_async_copy(sent, sent, z_send).wait()
    for i in range(3):
        pltpu.make_async_copy(other, other, y_send.at[i]).wait()
    for ys in range(4):
        pltpu.make_async_copy(other, other, sib_send.at[ys]).wait()
    for i in range(3):
        pltpu.make_async_copy(relay, relay, xs_send.at[i]).wait()
    three = score.at[pl.ds(0, 3)]
    pltpu.make_async_copy(three, three, dp_send).wait()
    store.wait()


def shards(grad_out, routes, probs, hidden, weight):
    dma = pltpu.SemaphoreType.DMA
    vmem, hbm = pl.BlockSpec(memory_space=pltpu.VMEM), pl.BlockSpec(memory_space=pl.ANY)
    grad_hidden, grad_probs = pl.pallas_call(
        kernel,
        out_shape=(
            jax.ShapeDtypeStruct((1, FFX, SLOTS), BF16),
            jax.ShapeDtypeStruct((2, TOK), F32),
        ),
        in_specs=[hbm, vmem, vmem, hbm, hbm],
        out_specs=(hbm, vmem),
        scratch_shapes=[
            pltpu.VMEM((TOK, D), BF16),
            pltpu.VMEM((Z, 16, MSG), BF16),
            pltpu.VMEM((Z, 16, MSG), BF16),
            pltpu.VMEM((PAIRS, 16, MSG), BF16),
            pltpu.VMEM((2, 4, PAIRS, 16, MSG), BF16),
            pltpu.VMEM((FP, D), BF16),
            pltpu.VMEM((FP, SLOTS), BF16),
            pltpu.VMEM((SLOTS, FP), F32),
            pltpu.VMEM((UNITS, 4, 24, FP), F32),
            pltpu.VMEM((UNITS, 24, FP), F32),
            pltpu.VMEM((2, UNITS, 24, FP), F32),
            pltpu.VMEM((SLOTS, FP), F32),
            pltpu.VMEM((FP, SLOTS), BF16),
            pltpu.VMEM((EXP, 1, TOK), F32),
            pltpu.VMEM((EXP, 1, TOK), F32),
            pltpu.VMEM((SLOTS, TOK), F32),
            pltpu.VMEM((4, UNITS, 1, TOK), F32),
            pltpu.VMEM((UNITS, 1, TOK), F32),
            pltpu.VMEM((EXP, 1, TOK), F32),
            pltpu.VMEM((TOK, TOK), F32),
            pltpu.VMEM((2, EXP, TOK), F32),
            pltpu.VMEM((2, 8, TOK), jnp.int32),
            dma((4,)),
            dma,
            dma((Z,)),
            dma((3,)),
            dma((4,)),
            dma((2, 4, PAIRS)),
            dma,
            dma,
            dma((3,)),
            dma((UNITS,)),
            dma((2, UNITS)),
            dma,
            dma((PAIRS,)),
            dma,
            dma,
        ],
        compiler_params=pltpu.CompilerParams(
            collective_id=0, has_side_effects=True, vmem_limit_bytes=60 * 1024 * 1024
        ),
        name="moe_down_backward",
    )(grad_out, routes.T, probs.T, jnp.swapaxes(hidden, 1, 2), weight)
    return jnp.swapaxes(grad_hidden, 1, 2), grad_probs.T


def solution(mesh):
    return jax.shard_map(
        shards,
        mesh=mesh,
        in_specs=(
            P(("dp", "expert"), "tensor"),
            P(("dp", "expert"), None),
            P(("dp", "expert"), None),
            P("expert", "tensor", "dp"),
            P("expert", "dp", "tensor"),
        ),
        out_specs=(P("expert", "tensor", "dp"), P(("dp", "expert"), None)),
        check_vma=False,
    )
```

time: 480 us -> 122 us (0.25); the launches traced: 473 us -> 121 us
  blocking collectives: 354 us -> 0 us
  Pallas kernels: 0 us -> 118 us
  waiting for transfers between devices: 43.1 us -> 0 us
  starting transfers between devices: 26.1 us -> 0 us
  local copies, waits for them, and re-layouts: 21.5 us -> 3.06 us
  between operations: 14.2 us -> 0.64 us
  matrix products: 11 us -> 0 us
    all_to_all x1 -> x0, blocking collectives: 339 us -> none  [shards(): lax.all_to_all(copies_dout, ('dp', 'expert'), split_axis=0, concat_axis=0...]
    pallas_call x0 -> x1, Pallas kernels: none -> 118 us  [shards(): pl.pallas_call(kernel, out_shape=(jax.ShapeDtypeStruct((1, FFX, SLOTS), B...]
    all_to_all x2 -> x0, starting transfers between devices: 26.1 us -> none  [the longest x1 13.3 us: shards(): lax.all_to_all(own_scores.reshape(expert_count, capacity), 'expert', spli...]
    all_to_all x2 -> x0, waiting for transfers between devices: 23.6 us -> none  [the longest x1 12.6 us: shards(): lax.all_to_all(copies_prob, ('dp', 'expert'), split_axis=0, concat_axis=0...]
    reduce_scatter x1 -> x0, waiting for transfers between devices: 19.5 us -> none  [shards(): lax.psum_scatter(jnp.einsum('sd,fd->sf', dout_rows, local_weight, preferr...]
    reshape x6 -> x0, local copies, waits for them, and re-layouts: 11.1 us -> none  [the longest x1 9.34 us: shards(): dout_rows = recv_dout.reshape(slots_all, -1)]
    dot_general x5 -> x0, matrix products: 11 us -> none  [the longest x1 7.93 us: shards(): jnp.einsum('sd,fd->sf', dout_rows, local_weight, preferred_element_type=j...]
    all_gather x1 -> x0, blocking collectives: 8.06 us -> none  [shards(): spread = lax.all_gather(summed, 'tensor', axis=0, tiled=True)]
  transfers between devices with their start and end apart: 3 -> 0, of which waited for: 3 -> 0; matrix products, arithmetic and copies ran while one was open for 0% -> 0% of each run, Pallas kernels for 0% -> 0%
where the time goes in v2:
time: 122 us; the launch traced here: 121 us
  Pallas kernels  118 us (97%)
  local copies, waits for them, and re-layouts  3.06 us (3%)
    pallas_call x1, Pallas kernels, shards(): pl.pallas_call(kernel, out_shape=(jax.ShapeDtypeStruct((1, FFX, SLOTS), B...  118 us
    unnamed x2, local copies, waits for them, and re-layouts  3.06 us

profile of v2, /device:TPU:25, one launch (start us, length us, event | category | flops | bytes accessed | tf_op | source)
XLA Modules:
  0.0 121.3 jit_solution(126602458969821636)
XLA Ops:
  0.6 117.6 %moe_down_backward.1 = (bf16[1,608,384]{2,1,0:T(8,128)(2,1)}, f32[2,128]{1,0:T(2,128)}) custom-call(bf16[128,1792]{1,0:T(8,128)(2,1)} %grad_hbm.1, s32[2,128]{1,0:T(2,128)} %bitcast.7, bf16[2,128]{1,0:T(2,128)(2,1)} %bitcast.9, bf16[1,608,384]{2,1,0:T(8,128)(2,1)} %bitcast.5, bf16[1,608,1792]{2,1,0:T(8,128)(2,1)} %weight_hbm.1), custom_call_target="tpu_custom_call" | custom-call | tf_op jit(solution)/shard_map/moe_down_backward/pallas_call | solution.py:382
  118.3 1.8 %copy.9 = bf16[1,384,608]{1,2,0:T(8,128)(2,1)} copy(bf16[1,384,608]{1,2,0:T(8,128)(2,1)} %bitcast.6) | data formatting | bytes 933888
  120.1 1.2 %copy.10 = f32[128,2]{0,1:T(2,128)} copy(f32[128,2]{0,1:T(2,128)} %bitcast.8) | data formatting | bytes 2048

commit v3 on v2

--- a/solution.py
+++ b/solution.py
@@ -5,10 +5,7 @@
 from jax.experimental.pallas import tpu as pltpu
 from jax.sharding import PartitionSpec as P
 
-ORDER = (0, 1, -1, 2, -2, 3, -3, 4)
-AHEAD = 3
-SEQ = "ZYCAFG"
-LAGS = dict(Z=0, Y=1, C=1, A=2, F=3, G=4)
+ORDER = (0, 1, -1, 3, -3, 4, 2, -2)
 MESH = pl.DeviceIdType.MESH
 F32 = jnp.float32
 BF16 = jnp.bfloat16
@@ -53,10 +50,10 @@
 def kernel(
     grad_hbm, routes_ref, probs_ref, hidden_hbm, weight_hbm,
     gh_hbm, gp_ref,
-    tokens, send, zbuf, other, recv, w_buf, h_buf, hidden, part, relay, fin, result, out_buf,
-    prob_out, prob_in, prob_col, score, score_sum, score_in, table, hot, slots,
-    local_sem, z_send, z_recv, y_send, sib_send, x_recv,
-    p_send, p_recv, xs_send, relay_recv, fin_recv, dp_send, dp_recv, s_send, s_recv,
+    tokens, send, zbuf, other, recv, w_buf, h_buf, natural, hidden, part, relay, fin, result, out_buf,
+    prob_out, prob_mid, prob_in, prob_col, score, group_in, score_sum, score_in, table, hot, slots,
+    local_sem, h_send, h_recv, z_send, z_recv, y_send, sib_send, x_recv,
+    p_send, p_recv, q_send, q_recv, xs_send, relay_recv, fin_recv, g_send, g_recv, s_send, s_recv,
 ):
     dp = lax.axis_index("dp")
     ex = lax.axis_index("expert")
@@ -65,13 +62,14 @@
     l, z = lax.div(ex, Z), lax.rem(ex, Z)
     y = 2 * h + l
     pair = lax.div(z, 2)
+    group = 4 * dp + x
     sibling = (2 * h + 1 - c, ex, x)
     opposite = (2 * (1 - h) + c, ex, x)
     beside = ((c, (1 - l) * Z + z, x), (2 + c, (1 - l) * Z + z, x))
 
     load_grad = pltpu.make_async_copy(grad_hbm, tokens, local_sem.at[0])
     load_w = pltpu.make_async_copy(weight_hbm.at[0], w_buf.at[pl.ds(0, FFX)], local_sem.at[1])
-    load_h = pltpu.make_async_copy(hidden_hbm.at[0], h_buf.at[pl.ds(0, FFX)], local_sem.at[2])
+    load_h = pltpu.make_async_copy(hidden_hbm.at[0], h_buf.at[x, pl.ds(0, FFX)], local_sem.at[2])
     load_grad.start()
     load_w.start()
     load_h.start()
@@ -81,28 +79,18 @@
     def greet(device):
         pl.semaphore_signal(barrier, inc=1, device_id=device, device_id_type=MESH)
 
-    def greet_z(i, carry):
-        greet((dp, l * Z + lax.rem(z + i, Z), x))
+    def greet_line(i, carry):
+        greet((dp, lax.rem(ex + i, EXP), x))
         return carry
 
-    lax.fori_loop(1, Z, greet_z, 0)
-    greet(sibling)
-    greet(opposite)
-    greet((2 * (1 - h) + 1 - c, ex, x))
-    greet(beside[0])
-    greet(beside[1])
-    for i in range(1, 4):
-        greet((dp, ex, lax.rem(x + i, 4)))
-    twin = x == dp
-
-    def greet_t(i, carry):
-        @pl.when(jnp.logical_or(jnp.logical_not(twin), i != ex))
-        def _():
-            greet((x, i, dp))
-
+    def greet_group(i, carry):
+        g = lax.rem(group + i, 16)
+        greet((lax.div(g, 4), ex, lax.rem(g, 4)))
         return carry
 
-    lax.fori_loop(0, EXP, greet_t, 0)
+    lax.fori_loop(1, EXP, greet_line, 0)
+    lax.fori_loop(1, 16, greet_group, 0)
+    greet((2 * (1 - h) + c, (1 - l) * Z + z, x))
 
     expert = iota((EXP, TOK), 0)
     hots = [(routes_ref[k : k + 1, :] == expert).astype(F32) for k in range(2)]
@@ -130,88 +118,116 @@
             halves.append(block.reshape(Z, 8, 128))
         send[:, :, D + n : D + n + 128] = jnp.concatenate(halves, axis=1).astype(BF16)
 
-    pl.semaphore_wait(barrier, jnp.where(twin, 54, 55))
-
-    def send_z(k):
-        for i in range(2):
-            to = 2 * lax.rem(pair + offset(k) + PAIRS, PAIRS) + i
-
-            @pl.when(to == z)
-            def _():
-                pltpu.make_async_copy(send.at[to], zbuf.at[z], z_recv.at[z]).start()
-
-            @pl.when(to != z)
-            def _():
-                pltpu.make_async_remote_copy(
-                    send.at[to], zbuf.at[z], z_send, z_recv.at[z],
-                    device_id=(dp, l * Z + to, x), device_id_type=MESH,
-                ).start()
-
-    def send_first(k, carry):
-        send_z(k)
-        return carry
-
-    lax.fori_loop(0, AHEAD, send_first, 0)
-
     def small(source, target, n, sent, got):
-        own = jnp.logical_and(twin, n == ex)
-
-        @pl.when(own)
+        @pl.when(n == ex)
         def _():
             pltpu.make_async_copy(source, target, got).start()
 
-        @pl.when(jnp.logical_not(own))
+        @pl.when(n != ex)
         def _():
             pltpu.make_async_remote_copy(
-                source, target, sent, got, device_id=(x, n, dp), device_id_type=MESH
+                source, target, sent, got, device_id=(dp, n, x), device_id_type=MESH
             ).start()
-
-    def small_sent(target, sent):
-        @pl.when(twin)
-        def _():
-            ref = target.at[pl.ds(0, EXP - 1)]
-            pltpu.make_async_copy(ref, ref, sent).wait()
-
-        @pl.when(jnp.logical_not(twin))
-        def _():
-            pltpu.make_async_copy(target, target, sent).wait()
 
     probs = probs_ref[...].astype(F32)
     weights = jnp.zeros((EXP, TOK), F32)
+    zz = lax.rem(z, 2)
     for k in range(2):
         at = jnp.sum(hots[k] * earlier, axis=0, keepdims=True).astype(jnp.int32)
         weights += dot_t(
             (hots[k] * probs[k : k + 1, :]).astype(BF16), (iota((TOK, TOK), 0) == at).astype(BF16)
         )
         hot[k] = hots[k]
-        slots[k] = jnp.broadcast_to(at + lax.rem(z, 2) * CAP, (8, TOK))
+        slots[k] = jnp.broadcast_to(jnp.where(at < 8, 8 * zz + at, 8 + 4 * zz + at), (8, TOK))
     for e in range(EXP):
         prob_out[e] = weights[e : e + 1, :]
+    load_h.wait()
+
+    pl.semaphore_wait(barrier, 47)
 
     def send_prob(n, carry):
-        small(prob_out.at[n], prob_in.at[ex], n, p_send, p_recv)
+        small(prob_out.at[n], prob_mid.at[ex], n, p_send, p_recv)
         return carry
 
     lax.fori_loop(0, EXP, send_prob, 0)
 
-    h_buf[FFX:FP, :] = jnp.zeros((FP - FFX, SLOTS), BF16)
+    def send_z(i, carry):
+        to = 2 * lax.rem(pair + offset(lax.div(i, 2)) + PAIRS, PAIRS) + lax.rem(i, 2)
+
+        @pl.when(to == z)
+        def _():
+            pltpu.make_async_copy(send.at[to], zbuf.at[z], z_recv.at[z]).start()
+
+        @pl.when(to != z)
+        def _():
+            pltpu.make_async_remote_copy(
+                send.at[to], zbuf.at[z], z_send, z_recv.at[z],
+                device_id=(dp, l * Z + to, x), device_id_type=MESH,
+            ).start()
+
+        return carry
+
+    lax.fori_loop(0, Z, send_z, 0)
+
+    own_hidden = h_buf.at[x, pl.ds(0, FFX)]
+    for i in range(1, 4):
+        pltpu.make_async_remote_copy(
+            own_hidden, own_hidden, h_send, h_recv.at[x],
+            device_id=(dp, ex, lax.rem(x + i, 4)), device_id_type=MESH,
+        ).start()
     w_buf[FFX:FP, :] = jnp.zeros((FP - FFX, D), BF16)
+    for i in range(4):
+        h_buf[i, FFX:FP, :] = jnp.zeros((FP - FFX, SLOTS), BF16)
     table[...] = jnp.zeros((TOK, TOK), F32)
-    load_h.wait()
-    for i in range(0, SLOTS, 128):
-        for j in range(0, FP, 128):
-            hidden[i : i + 128, j : j + 128] = jnp.transpose(h_buf[j : j + 128, i : i + 128].astype(F32))
     load_w.wait()
 
+    def take_hidden(xs, carry):
+        @pl.when(xs != x)
+        def _():
+            ref = h_buf.at[xs, pl.ds(0, FFX)]
+            pltpu.make_async_copy(ref, ref, h_recv.at[xs]).wait()
+
+        for i in range(0, SLOTS, 128):
+            for j in range(0, FP, 128):
+                natural[i : i + 128, j : j + 128] = jnp.transpose(
+                    h_buf[xs, j : j + 128, i : i + 128].astype(F32)
+                )
+
+        def permute(u, inner):
+            rows = pl.multiple_of(24 * u, 8)
+            low = iota((8, FP), 0) < 4
+            a, b = natural[pl.ds(rows + 8, 8), :], natural[pl.ds(rows + 16, 8), :]
+            hidden[xs, pl.ds(rows, 8), :] = natural[pl.ds(rows, 8), :]
+            hidden[xs, pl.ds(rows + 8, 8), :] = jnp.where(low, pltpu.roll(a, 4, 0), pltpu.roll(b, 4, 0))
+            hidden[xs, pl.ds(rows + 16, 8), :] = jnp.where(low, a, b)
+            return inner
+
+        return lax.fori_loop(0, UNITS, permute, carry)
+
+    def pass_prob():
+        pltpu.make_async_copy(prob_mid, prob_mid, p_recv).wait()
+
+        @pl.when(x == dp)
+        def _():
+            pltpu.make_async_copy(prob_mid, prob_in, q_recv).start()
+
+        @pl.when(x != dp)
+        def _():
+            pltpu.make_async_remote_copy(
+                prob_mid, prob_in, q_send, q_recv, device_id=(x, ex, dp), device_id_type=MESH
+            ).start()
+
     def take_prob():
-        pltpu.make_async_copy(prob_in, prob_in, p_recv).wait()
+        pltpu.make_async_copy(prob_in, prob_in, q_recv).wait()
         for e in range(EXP):
             table[e : e + 1, :] = prob_in[e]
         row, col = iota((SLOTS, EXP), 0), iota((SLOTS, EXP), 1)
         spread = dot(((row * 5462) >> 16 == col).astype(BF16), table[0:EXP].astype(BF16))
         row, col = iota((SLOTS, TOK), 0), iota((SLOTS, TOK), 1)
         mine = row - CAP * ((row * 5462) >> 16) == col
-        prob_col[...] = jnp.broadcast_to(jnp.sum(jnp.where(mine, spread, 0.0), axis=1, keepdims=True), (SLOTS, TOK))
+        prob_col[...] = jnp.broadcast_to(
+            jnp.sum(jnp.where(mine, spread, 0.0), axis=1, keepdims=True), (SLOTS, TOK)
+        )
 
     def origin(k):
         return lax.rem(pair - offset(k) + PAIRS, PAIRS)
@@ -287,8 +303,8 @@
             u = 2 * rp + lo
             to = lax.rem(x + turn(lo), 4)
             pltpu.make_async_copy(relay.at[u], relay.at[u], relay_recv.at[u]).wait()
-            part[u, to] = part[u, to] + relay[u]
-            along_x(2, part.at[u, to], fin.at[0, u], fin_recv.at[0, u], to)
+            relay[u] = part[u, to] + relay[u]
+            along_x(2, relay.at[u], fin.at[0, u], fin_recv.at[0, u], to)
 
     def finish(k):
         rp = origin(k)
@@ -304,47 +320,67 @@
             )
             rows = pl.ds(pl.multiple_of(192 * lo + 24 * rp, 8), 24)
             result[rows, :] = prob_col[rows, 0:1] * total
-            col = jnp.sum(hidden[rows, :] * total, axis=1, keepdims=True)
-            score[dp, u] = jnp.sum(
-                jnp.where(iota((24, TOK), 0) == iota((24, TOK), 1), col, 0.0), axis=0, keepdims=True
-            )
-        ref = score.at[dp, pl.ds(2 * rp, 2)]
-        for i in range(1, 4):
-            pltpu.make_async_remote_copy(
-                ref, ref, dp_send, dp_recv.at[rp], device_id=(lax.rem(dp + i, 4), ex, x), device_id_type=MESH
-            ).start()
-
-    def give(k):
-        rp = origin(k)
-        three = score.at[0, pl.ds(0, 6)]
-        pltpu.make_async_copy(three, three, dp_recv.at[rp]).wait()
+
+    def scores(k):
+        rp = origin(k)
         for lo in range(2):
             u = 2 * rp + lo
-            score_sum[u] = (score[0, u] + score[1, u]) + (score[2, u] + score[3, u])
+            rows = pl.ds(pl.multiple_of(192 * lo + 24 * rp, 8), 24)
+            for d in range(4):
+                col = jnp.sum(hidden[d, rows, :] * part[u, d], axis=1, keepdims=True)
+                score[d, u] = jnp.sum(
+                    jnp.where(iota((24, TOK), 0) == iota((24, TOK), 1), col, 0.0), axis=0, keepdims=True
+                )
+            group_in[group, u] = score[dp, u]
+
+        def exchange(i, carry):
+            g = lax.rem(group + i, 16)
+            to = lax.div(g, 4)
+            pltpu.make_async_remote_copy(
+                score.at[to, pl.ds(2 * rp, 2)], group_in.at[group, pl.ds(2 * rp, 2)], g_send, g_recv.at[rp],
+                device_id=(to, ex, lax.rem(g, 4)), device_id_type=MESH,
+            ).start()
+            return carry
+
+        lax.fori_loop(1, 16, exchange, 0)
+
+    def give(k):
+        rp = origin(k)
+        others = group_in.at[pl.ds(0, 15), pl.ds(0, 2)]
+        pltpu.make_async_copy(others, others, g_recv.at[rp]).wait()
+        for lo in range(2):
+            u = 2 * rp + lo
+            rows = [group_in[g, u] for g in range(16)]
+            while len(rows) > 1:
+                rows = [a + b for a, b in zip(rows[::2], rows[1::2], strict=True)]
+            score_sum[u] = rows[0]
             for i in range(2):
                 small(score_sum.at[u], score_in.at[ex], lo * Z + 2 * rp + i, s_send, s_recv)
 
-    named = dict(Z=stage_z, Y=stage_y, C=compute, A=add_x, F=finish, G=give)
-    stages = [(named[n], LAGS[n]) for n in SEQ]
-
     def step(k, carry):
-        @pl.when(k < PAIRS - AHEAD)
-        def _():
-            send_z(k + AHEAD)
-
-        @pl.when(k == LAGS["F"] - 1)
-        def _():
-            take_prob()
-
-        for stage, lag in stages:
-
-            @pl.when(jnp.logical_and(k >= lag, k < PAIRS + lag))
-            def _(stage=stage, lag=lag):
-                stage(k - lag)
-
+        def at(first, last, stage, *args):
+            @pl.when(jnp.logical_and(k >= first, k <= last))
+            def _():
+                stage(*args)
+
+        last = PAIRS - 1
+        at(1, 1, pass_prob)
+        at(2, 2, take_prob)
+        at(3, 3, lambda: lax.fori_loop(0, 4, take_hidden, 0))
+        at(0, last, stage_z, k)
+        at(1, last + 1, stage_y, k - 1)
+        at(1, last + 1, compute, k - 1)
+        at(3, 3, scores, k - 3)
+        at(3, 3, scores, k - 2)
+        at(3, last + 1, scores, k - 1)
+        at(4, 4, give, k - 4)
+        at(4, 4, give, k - 3)
+        at(4, last + 2, give, k - 2)
+        at(2, last + 2, add_x, k - 2)
+        at(3, last + 3, finish, k - 3)
         return carry
 
-    lax.fori_loop(0, PAIRS + max(LAGS.values()), step, 0)
+    lax.fori_loop(0, PAIRS + 3, step, 0)
 
     for i in range(0, SLOTS, 128):
         for j in range(0, FP, 128):
@@ -361,8 +397,16 @@
         mine = iota((TOK, TOK), 0) == slots[k, 0:1, :]
         gp_ref[k : k + 1, :] = jnp.sum(jnp.where(mine, spread, 0.0), axis=0, keepdims=True)
 
-    small_sent(prob_in, p_send)
-    small_sent(score_in, s_send)
+    for ref, sem in ((prob_mid, p_send), (score_in, s_send)):
+        ref = ref.at[pl.ds(0, EXP - 1)]
+        pltpu.make_async_copy(ref, ref, sem).wait()
+
+    @pl.when(x != dp)
+    def _():
+        pltpu.make_async_copy(prob_mid, prob_mid, q_send).wait()
+
+    ref = h_buf.at[pl.ds(0, 3), pl.ds(0, FFX)]
+    pltpu.make_async_copy(ref, ref, h_send).wait()
     sent = send.at[pl.ds(0, Z - 1)]
     pltpu.make_async_copy(sent, sent, z_send).wait()
     for i in range(3):
@@ -371,8 +415,8 @@
         pltpu.make_async_copy(other, other, sib_send.at[ys]).wait()
     for i in range(3):
         pltpu.make_async_copy(relay, relay, xs_send.at[i]).wait()
-    three = score.at[pl.ds(0, 3)]
-    pltpu.make_async_copy(three, three, dp_send).wait()
+    others = group_in.at[pl.ds(0, 15)]
+    pltpu.make_async_copy(others, others, g_send).wait()
     store.wait()
 
 
@@ -394,8 +438,9 @@
             pltpu.VMEM((PAIRS, 16, MSG), BF16),
             pltpu.VMEM((2, 4, PAIRS, 16, MSG), BF16),
             pltpu.VMEM((FP, D), BF16),
-            pltpu.VMEM((FP, SLOTS), BF16),
+            pltpu.VMEM((4, FP, SLOTS), BF16),
             pltpu.VMEM((SLOTS, FP), F32),
+            pltpu.VMEM((4, SLOTS, FP), F32),
             pltpu.VMEM((UNITS, 4, 24, FP), F32),
             pltpu.VMEM((UNITS, 24, FP), F32),
             pltpu.VMEM((2, UNITS, 24, FP), F32),
@@ -403,8 +448,10 @@
             pltpu.VMEM((FP, SLOTS), BF16),
             pltpu.VMEM((EXP, 1, TOK), F32),
             pltpu.VMEM((EXP, 1, TOK), F32),
+            pltpu.VMEM((EXP, 1, TOK), F32),
             pltpu.VMEM((SLOTS, TOK), F32),
             pltpu.VMEM((4, UNITS, 1, TOK), F32),
+            pltpu.VMEM((16, UNITS, 1, TOK), F32),
             pltpu.VMEM((UNITS, 1, TOK), F32),
             pltpu.VMEM((EXP, 1, TOK), F32),
             pltpu.VMEM((TOK, TOK), F32),
@@ -412,10 +459,14 @@
             pltpu.VMEM((2, 8, TOK), jnp.int32),
             dma((4,)),
             dma,
+            dma((4,)),
+            dma,
             dma((Z,)),
             dma((3,)),
             dma((4,)),
             dma((2, 4, PAIRS)),
+            dma,
+            dma,
             dma,
             dma,
             dma((3,)),

time: 122 us -> 113 us (0.926)
  the two profiles are of different devices: /device:TPU:25 before, /device:TPU:64 now
where the time goes in v3:
time: 113 us
  Pallas kernels  109 us (96%)
  local copies, waits for them, and re-layouts  3.06 us (3%)
    pallas_call x1, Pallas kernels, shards(): pl.pallas_call(kernel, out_shape=(jax.ShapeDtypeStruct((1, FFX, SLOTS), B...  109 us
    unnamed x2, local copies, waits for them, and re-layouts  3.06 us

profile of v3, /device:TPU:64, one launch (start us, length us, event | category | flops | bytes accessed | tf_op | source)
XLA Modules:
  0.0 113.1 jit_solution(595975650576871745)
XLA Ops:
  0.6 109.4 %moe_down_backward.1 = (bf16[1,608,384]{2,1,0:T(8,128)(2,1)}, f32[2,128]{1,0:T(2,128)}) custom-call(bf16[128,1792]{1,0:T(8,128)(2,1)} %grad_hbm.1, s32[2,128]{1,0:T(2,128)} %bitcast.7, bf16[2,128]{1,0:T(2,128)(2,1)} %bitcast.9, bf16[1,608,384]{2,1,0:T(8,128)(2,1)} %bitcast.5, bf16[1,608,1792]{2,1,0:T(8,128)(2,1)} %weight_hbm.1), custom_call_target="tpu_custom_call" | custom-call | tf_op jit(solution)/shard_map/moe_down_backward/pallas_call | solution.py:426
  110.0 1.8 %copy.9 = bf16[1,384,608]{1,2,0:T(8,128)(2,1)} copy(bf16[1,384,608]{1,2,0:T(8,128)(2,1)} %bitcast.6) | data formatting | bytes 933888
  111.8 1.2 %copy.10 = f32[128,2]{0,1:T(2,128)} copy(f32[128,2]{0,1:T(2,128)} %bitcast.8) | data formatting | bytes 2048

commit v4 on v3

--- a/solution.py
+++ b/solution.py
@@ -5,7 +5,7 @@
 from jax.experimental.pallas import tpu as pltpu
 from jax.sharding import PartitionSpec as P
 
-ORDER = (0, 1, -1, 3, -3, 4, 2, -2)
+ORDER = (0, 1, -1, 3, -3, 2, 4, -2)
 MESH = pl.DeviceIdType.MESH
 F32 = jnp.float32
 BF16 = jnp.bfloat16

time: 113 us -> 113 us (level)
  the two profiles are of different devices: /device:TPU:64 before, /device:TPU:96 now
where the time goes in v4:
time: 113 us
  Pallas kernels  109 us (96%)
  local copies, waits for them, and re-layouts  3.06 us (3%)
    pallas_call x1, Pallas kernels, shards(): pl.pallas_call(kernel, out_shape=(jax.ShapeDtypeStruct((1, FFX, SLOTS), B...  109 us
    unnamed x2, local copies, waits for them, and re-layouts  3.06 us

profile of v4, /device:TPU:96, one launch (start us, length us, event | category | flops | bytes accessed | tf_op | source)
XLA Modules:
  0.0 112.6 jit_solution(12810088263563681170)
XLA Ops:
  0.6 108.9 %moe_down_backward.1 = (bf16[1,608,384]{2,1,0:T(8,128)(2,1)}, f32[2,128]{1,0:T(2,128)}) custom-call(bf16[128,1792]{1,0:T(8,128)(2,1)} %grad_hbm.1, s32[2,128]{1,0:T(2,128)} %bitcast.7, bf16[2,128]{1,0:T(2,128)(2,1)} %bitcast.9, bf16[1,608,384]{2,1,0:T(8,128)(2,1)} %bitcast.5, bf16[1,608,1792]{2,1,0:T(8,128)(2,1)} %weight_hbm.1), custom_call_target="tpu_custom_call" | custom-call | tf_op jit(solution)/shard_map/moe_down_backward/pallas_call | solution.py:426
  109.5 1.8 %copy.9 = bf16[1,384,608]{1,2,0:T(8,128)(2,1)} copy(bf16[1,384,608]{1,2,0:T(8,128)(2,1)} %bitcast.6) | data formatting | bytes 933888
  111.4 1.2 %copy.10 = f32[128,2]{0,1:T(2,128)} copy(f32[128,2]{0,1:T(2,128)} %bitcast.8) | data formatting | bytes 2048
